TPU v7x, 256 devices: a whole 4x4x8 slice. The times are simulated.
256 devices in a mesh: dp: 32 (over z, x), tensor: 8 (over y, core).
Axes of the slice: x: 4, y: 4, z: 8, core: 2. Of those that a mesh axis runs over, the one named last changes fastest.
Arguments:
- activations: bfloat16 [28672, 4096], P('dp', 'tensor'), may hold values from -6 to 6
- out_grads: bfloat16 [28672, 4096], P('dp', 'tensor'), may hold values from -6 to 6
- gate_act: bfloat16 [28672, 14336], P('dp', 'tensor'), may hold values from -6 to 6
- w_down: bfloat16 [14336, 4096], P('tensor', 'dp'), may hold values from -0.09375 to 0.09375
- proj_in: bfloat16 [4096, 64], P('tensor'), may hold values from -0.09375 to 0.09375
- proj_out: bfloat16 [14336, 64], P('tensor'), may hold values from -0.046875 to 0.046875
- lengths: int32 [32, 8], P('dp'), may hold values from 1 to 448, 896 in all within a row
- assign: int32 [256], replicated, may hold values from 0 to 255, each once
Outputs:
- loggrads: float32 [256, 64, 64], P('dp', 'tensor')
Inputs may be any that keep to these rules, and one draw needn't show every extreme that they name: `lengths`: each row gives the token counts of the 8 sequences packed into one data group's 896 rows and sums to 896. `assign`: a permutation of the sequence numbers.
All inputs are finite; a program needn't handle non-finite values.
Results may differ from a plain program's by a relative error of at most 0.013.
Values may be sent and summed in bfloat16 or wider, within the bound.
No kernel may reach another device: no remote copies, remote signals or barrier semaphores. Data moves between devices by JAX's collectives and lax.ppermute only.
A program may use at most 128 MiB of HBM per device.

v0:
```python
import jax
import jax.numpy as jnp
from jax import lax
from jax.sharding import PartitionSpec as P


def member_of(seq_lengths, tok_rows):
    slots = seq_lengths.shape[0]
    before = lax.iota(jnp.int32, slots)[None, :] < lax.iota(jnp.int32, slots)[:, None]
    starts = jnp.sum(jnp.where(before, seq_lengths[None, :], 0), axis=1)
    ends = starts + seq_lengths
    positions = lax.iota(jnp.int32, tok_rows)
    inside = (positions[None, :] >= starts[:, None]) & (positions[None, :] < ends[:, None])
    return jnp.where(inside, 1.0 / seq_lengths[:, None].astype(jnp.float32), 0.0)


def place(result, assign):
    slots, values = result.shape
    groups = lax.axis_size("dp")
    mine = lax.dynamic_slice_in_dim(assign, lax.axis_index("dp") * slots, slots, 0)
    placing = (mine[None, :] == lax.iota(jnp.int32, slots * groups)[:, None]).astype(jnp.bfloat16)
    spread = jnp.dot(placing, result, preferred_element_type=jnp.float32).astype(jnp.bfloat16)
    got = lax.all_to_all(spread, "dp", split_axis=0, concat_axis=0, tiled=True)
    return jnp.sum(got.reshape(groups, slots, values).astype(jnp.float32), axis=0)


def shards(activations, out_grads, gate_act, w_down, proj_in, proj_out, lengths, assign):
    tok_rows = activations.shape[0]
    rank_all = proj_in.shape[1]
    shard_count = lax.axis_size("tensor")
    slots = lengths.shape[1]
    cols = rank_all // shard_count
    in_part = jnp.dot(activations, proj_in, preferred_element_type=jnp.float32)
    in_high = in_part.astype(jnp.bfloat16)
    in_low = (in_part - in_high.astype(jnp.float32)).astype(jnp.bfloat16)
    full_grads = lax.all_gather(out_grads, "tensor", axis=1, tiled=True)
    in_all = lax.all_gather(jnp.concatenate([in_high, in_low], axis=1), "tensor", axis=0)
    in_all = jnp.sum(in_all.astype(jnp.float32), axis=0)
    in_sum = in_all[:, :rank_all] + in_all[:, rank_all:]
    weighted = member_of(lengths[0], tok_rows)[:, :, None] * in_sum[None, :, :]
    hidden_grad = lax.dot_general(
        full_grads,
        lax.all_gather(w_down, "dp", axis=1, tiled=True),
        (((1,), (1,)), ((), ())),
        preferred_element_type=jnp.float32,
    )
    up_grad = (hidden_grad * gate_act.astype(jnp.float32)).astype(jnp.bfloat16)
    out_part = jnp.dot(up_grad, proj_out, preferred_element_type=jnp.float32)
    part = jnp.einsum("ctp,tq->cpq", weighted, out_part, precision=lax.Precision.HIGHEST)
    part = part.reshape(slots, shard_count, cols * rank_all).transpose(1, 0, 2)
    result = jnp.sum(
        lax.all_to_all(part, "tensor", split_axis=0, concat_axis=0, tiled=True), axis=0
    )
    return place(result.astype(jnp.bfloat16), assign).reshape(slots, cols, rank_all)


def solution(mesh):
    in_specs = (
        P("dp", "tensor"),
        P("dp", "tensor"),
        P("dp", "tensor"),
        P("tensor", "dp"),
        P("tensor", None),
        P("tensor", None),
        P("dp", None),
        P(),
    )
    out_specs = P("dp", "tensor", None)
    return jax.shard_map(shards, mesh=mesh, in_specs=in_specs, out_specs=out_specs, check_vma=False)
```

profile of v0, /device:TPU:32, one launch (start us, length us, event | category | flops | bytes accessed | tf_op | source)
XLA Modules:
  0.0 291.1 jit_solution(1241002359419916471)
XLA Ops:
  6.5 0.0 copy-start
  6.5 0.0 all-gather.9.cloned.1.call-start
  6.5 1.2 copy-done
  7.7 1.3 subtract_convert_fusion
  9.0 0.7 pad_maximum_fusion
  9.7 0.0 all-gather.9.cloned.1.call-update
  9.7 0.0 all-gather.5.cloned.1.call-start
  9.8 0.7 all-gather.5.cloned.1.call-update
  10.5 0.0 all-gather.7.cloned.1.call-start
  10.5 0.7 all-gather.7.cloned.1.call-update
  11.2 0.8 select_reduce_fusion
  12.0 0.7 convert_divide_fusion
  12.7 0.7 bitcast_add_fusion
  13.3 0.1 fusion.9
  13.4 26.7 %all-gather.9.cloned.1.call-done = bf16[7168,128]{0,1:T(8,128)(2,1)} async-done(((bf16[896,128]{0,1:T(8,128)(2,1)}), bf16[7168,128]{0,1:T(8,128)(2,1)}) %all-gather.9.cloned.1.call-update) | async-done | bytes 1835024 | tf_op jit(solution)/shard_map/all_gather | solution.py:37
  40.1 1.9 convert_element_type.46
  42.0 0.0 copy-start.1
  42.0 0.6 copy.11
  42.7 0.9 bitcast_reduce_fusion
  43.6 0.0 copy-start.2
  43.6 46.3 %all-gather.5.cloned.1.call-done = bf16[896,4096]{1,0:T(8,128)(2,1)} async-done(((bf16[896,512]{1,0:T(8,128)(2,1)}), bf16[896,4096]{1,0:T(8,128)(2,1)}) %all-gather.5.cloned.1.call-update) | async-done | bytes 7340048 | tf_op jit(solution)/shard_map/all_gather | solution.py:36
  89.8 141.1 %all-gather.7.cloned.1.call-done = bf16[1792,4096]{1,0:T(8,128)(2,1)} async-done(((bf16[1792,128]{1,0:T(8,128)(2,1)}), bf16[1792,4096]{1,0:T(8,128)(2,1)}) %all-gather.7.cloned.1.call-update) | async-done | bytes 14680080 | tf_op jit(solution)/shard_map/all_gather | solution.py:43
  230.9 0.0 copy-done.1
  230.9 22.0 %fusion.4 = f32[896,64,1]{0,1,2:T(8,128)S(1)} fusion(bf16[1792,64]{0,1:T(8,128)(2,1)S(1)} %copy-done.1, bf16[896,1792]{1,0:T(8,128)(2,1)} %param.10, bf16[896,4096]{1,0:T(8,128)(2,1)} %all-gather.5.cloned.1.call-done, bf16[1792,4096]{1,0:T(8,128)(2,1)} %all-gather.7.cloned.1.call-done), kind=kOutput, calls=%fused_computation.7 | convolution fusion | flops 13363675136 | bytes 25690112 | tf_op jit(solution)/shard_map/dot_general | solution.py:48
  253.0 1.7 fusion.1
  254.6 0.1 reshape.85
  254.8 0.7 copy.13
  255.5 4.3 %all-to-all-start = ((f32[8,8,512]{2,1,0:T(8,128)}), f32[8,8,512]{2,1,0:T(8,128)S(1)}, u32[]{:S(2)}, u32[]{:S(2)}) async-start(f32[8,8,512]{2,1,0:T(8,128)} %bitcast.21), calls=%async_computation | async-start | bytes 262144 | tf_op jit(solution)/shard_map/all_to_all | solution.py:52
  259.8 0.0 copy-done.2
  259.8 0.1 dynamic_slice.3
  259.8 6.1 %all-to-all-done = f32[8,8,512]{2,1,0:T(8,128)S(1)} async-done(((f32[8,8,512]{2,1,0:T(8,128)}), f32[8,8,512]{2,1,0:T(8,128)S(1)}, u32[]{:S(2)}, u32[]{:S(2)}) %all-to-all-start) | async-done | bytes 131104 | tf_op jit(solution)/shard_map/all_to_all | solution.py:52
  265.9 0.2 fusion.3
  266.1 17.7 %all_to_all.14 = bf16[32,8,512]{2,1,0:T(8,128)(2,1)S(1)} all-to-all(bf16[32,8,512]{2,1,0:T(8,128)(2,1)S(1)} %fusion.3), channel_id=1, replica_groups=mesh['dp'=32,'tensor'=8] {'dp'}, dimensions={0} | all-to-all | bytes 524288 | tf_op jit(solution)/shard_map/all_to_all | solution.py:23
  283.9 0.7 reshape.86
  (3 shorter events, 0.1 us)
Async XLA Ops:
  6.5 1.2 copy-start
  6.5 33.6 %all-gather.9.cloned.1.call-start = ((), (), s32[]{:S(2)}) async-start(), calls=%async_computation.4 | async-start | bytes 2064384 | tf_op jit(solution)/shard_map/all_gather | solution.py:37
  9.7 80.1 %all-gather.5.cloned.1.call-start = ((), (), s32[]{:S(2)}) async-start(), calls=%async_computation.2 | async-start | bytes 8257536 | tf_op jit(solution)/shard_map/all_gather | solution.py:36
  10.5 220.4 %all-gather.7.cloned.1.call-start = ((), (), s32[]{:S(2)}) async-start(), calls=%async_computation.3 | async-start | bytes 15138816 | tf_op jit(solution)/shard_map/all_gather | solution.py:43
  42.0 188.9 %copy-start.1 = (bf16[1792,64]{0,1:T(8,128)(2,1)S(1)}, bf16[1792,64]{0,1:T(8,128)(2,1)}, u32[]{:S(2)}) copy-start(bf16[1792,64]{0,1:T(8,128)(2,1)} %param.13) | copy-start | bytes 688132
  43.6 216.2 %copy-start.2 = (s32[256]{0:T(256)S(1)}, s32[256]{0:T(256)}, u32[]{:S(2)}) copy-start(s32[256]{0:T(256)} %param.15) | copy-start | bytes 3076
  255.5 10.4 %all-to-all-start = ((f32[8,8,512]{2,1,0:T(8,128)}), f32[8,8,512]{2,1,0:T(8,128)S(1)}, u32[]{:S(2)}, u32[]{:S(2)}) async-start(f32[8,8,512]{2,1,0:T(8,128)} %bitcast.21), calls=%async_computation | async-start | bytes 262144 | tf_op jit(solution)/shard_map/all_to_all | solution.py:52
Sparse Core Ops, SparseCore 0:
  9.9 30.2 all-gather.8
  42.0 47.8 all-gather.4
  92.3 138.5 all-gather.6
where the time goes:
time: 291 us
  waiting for transfers between devices  222 us (76%)
  matrix products  25.2 us (9%)
  blocking collectives  17.7 us (6%)
  between operations  13.2 us (5%)
  other arithmetic  5.72 us (2%)
  starting transfers between devices  4.37 us (2%)
  local copies, waits for them, and re-layouts  3.43 us (1%)
    all_gather x1, waiting for transfers between devices, shards(): lax.all_gather(w_down, 'dp', axis=1, tiled=True)  141 us
    all_gather x1, waiting for transfers between devices, shards(): full_grads = lax.all_gather(out_grads, 'tensor', axis=1, tiled=True)  46.3 us
    all_gather x1, waiting for transfers between devices, shards(): lax.all_gather(jnp.concatenate([in_high, in_low], axis=1), 'tensor', axis=0)  26.7 us
    dot_general x1, matrix products, shards(): out_part = jnp.dot(up_grad, proj_out, preferred_element_type=jnp.float32)  22 us
    all_to_all x1, blocking collectives, place(): got = lax.all_to_all(spread, 'dp', split_axis=0, concat_axis=0, tiled=True)  17.7 us
    all_to_all x1, waiting for transfers between devices, shards(): lax.all_to_all(part, 'tensor', split_axis=0, concat_axis=0, tiled=True)  6.05 us
  transfers between devices with their start and end apart: 4, of which 4 were waited for; matrix products, arithmetic and copies ran while one was open for 2% of the time, Pallas kernels for 0%

commit v1 on v0

--- a/solution.py
+++ b/solution.py
@@ -2,6 +2,16 @@
 import jax.numpy as jnp
 from jax import lax
 from jax.sharding import PartitionSpec as P
+
+store_the_modes = lambda slab_in, named_axis: jnp.concatenate(
+    jax.lax.all_to_all(
+        jnp.stack([slab_in] * jax.lax.axis_size(named_axis), 0),
+        axis_name=named_axis,
+        split_axis=0,
+        concat_axis=0,
+    ),
+    1,
+)
 
 
 def member_of(seq_lengths, tok_rows):
@@ -33,7 +43,7 @@
     in_part = jnp.dot(activations, proj_in, preferred_element_type=jnp.float32)
     in_high = in_part.astype(jnp.bfloat16)
     in_low = (in_part - in_high.astype(jnp.float32)).astype(jnp.bfloat16)
-    full_grads = lax.all_gather(out_grads, "tensor", axis=1, tiled=True)
+    full_grads = store_the_modes(out_grads, "tensor")
     in_all = lax.all_gather(jnp.concatenate([in_high, in_low], axis=1), "tensor", axis=0)
     in_all = jnp.sum(in_all.astype(jnp.float32), axis=0)
     in_sum = in_all[:, :rank_all] + in_all[:, rank_all:]

time: 291 us -> 253 us (0.87)
  waiting for transfers between devices: 222 us -> 174 us
  local copies, waits for them, and re-layouts: 3.43 us -> 8.88 us
  starting transfers between devices: 4.37 us -> 9.31 us
    all_gather x1, waiting for transfers between devices: 141 us -> 80.2 us  [shards(): lax.all_gather(w_down, 'dp', axis=1, tiled=True)]
    all_to_all x0 -> x1, waiting for transfers between devices: none -> 55.9 us  [jax.lax.all_to_all(jnp.stack([slab_in] * jax.lax.axis_size(named_axis), 0...]
    all_gather x1 -> x0, waiting for transfers between devices: 46.3 us -> none  [shards(): full_grads = lax.all_gather(out_grads, 'tensor', axis=1, tiled=True)]
    all_to_all x0 -> x1, starting transfers between devices: none -> 4.97 us  [jax.lax.all_to_all(jnp.stack([slab_in] * jax.lax.axis_size(named_axis), 0...]
    all_gather x1, waiting for transfers between devices: 26.7 us -> 31.2 us  [shards(): lax.all_gather(jnp.concatenate([in_high, in_low], axis=1), 'tensor', axis=0)]
    another operation x0 -> x1, local copies, waits for them, and re-layouts: none -> 3.91 us  [jnp.stack([slab_in] * jax.lax.axis_size(named_axis), 0)]
  transfers between devices with their start and end apart: 4 -> 4, of which waited for: 4 -> 4; matrix products, arithmetic and copies ran while one was open for 2% -> 4% of each run, Pallas kernels for 0% -> 0%
where the time goes in v1:
time: 253 us; the launch traced here: 252 us
  waiting for transfers between devices  174 us (69%)
  matrix products  25.2 us (10%)
  blocking collectives  17.7 us (7%)
  between operations  13.5 us (5%)
  starting transfers between devices  9.31 us (4%)
  local copies, waits for them, and re-layouts  8.88 us (4%)
  other arithmetic  3.73 us (1%)
    all_gather x1, waiting for transfers between devices, shards(): lax.all_gather(w_down, 'dp', axis=1, tiled=True)  80.2 us
    all_to_all x1, waiting for transfers between devices, jax.lax.all_to_all(jnp.stack([slab_in] * jax.lax.axis_size(named_axis), 0...  55.9 us
    all_gather x1, waiting for transfers between devices, shards(): lax.all_gather(jnp.concatenate([in_high, in_low], axis=1), 'tensor', axis=0)  31.2 us
    dot_general x1, matrix products, shards(): out_part = jnp.dot(up_grad, proj_out, preferred_element_type=jnp.float32)  22.1 us
    all_to_all x1, blocking collectives, place(): got = lax.all_to_all(spread, 'dp', split_axis=0, concat_axis=0, tiled=True)  17.7 us
    all_to_all x1, waiting for transfers between devices, shards(): lax.all_to_all(part, 'tensor', split_axis=0, concat_axis=0, tiled=True)  6.05 us
  transfers between devices with their start and end apart: 4, of which 4 were waited for; matrix products, arithmetic and copies ran while one was open for 4% of the time, Pallas kernels for 0%

profile of v1, /device:TPU:32, one launch (start us, length us, event | category | flops | bytes accessed | tf_op | source)
XLA Modules:
  0.0 252.4 jit_solution(1593732881167011636)
XLA Ops:
  6.5 0.0 copy-start
  6.5 0.0 all-gather.6.cloned.1.call-start
  6.5 1.2 copy-done
  7.7 1.3 subtract_convert_fusion
  9.0 0.7 pad_maximum_fusion
  9.7 0.0 all-gather.6.cloned.1.call-update
  9.7 0.0 all-gather.4.cloned.1.call-start
  9.8 0.7 all-gather.4.cloned.1.call-update
  10.5 1.5 copy.12
  12.0 3.9 %stack.2 = bf16[8,896,512]{1,2,0:T(8,128)(2,1)} broadcast(bf16[896,512]{0,1:T(8,128)(2,1)S(1)} %copy.12), dimensions={1,2} | broadcast | bytes 8257536 | tf_op jit(solution)/shard_map/stack | solution.py:8
  15.9 0.0 copy-start.3
  15.9 5.0 %all-to-all-start = ((bf16[8,896,512]{1,2,0:T(8,128)(2,1)}), bf16[8,896,512]{1,2,0:T(8,128)(2,1)}, u32[]{:S(2)}, u32[]{:S(2)}) async-start(bf16[8,896,512]{1,2,0:T(8,128)(2,1)} %stack.2), calls=%async_computation | async-start | bytes 14680064 | tf_op jit(solution)/shard_map/all_to_all | solution.py:7
  20.9 0.0 copy-done.3
  20.9 0.1 select_reduce_fusion
  21.1 0.1 fusion.9
  21.1 31.2 %all-gather.6.cloned.1.call-done = bf16[7168,128]{0,1:T(8,128)(2,1)} async-done(((bf16[896,128]{0,1:T(8,128)(2,1)}), bf16[7168,128]{0,1:T(8,128)(2,1)}) %all-gather.6.cloned.1.call-update) | async-done | bytes 1835024 | tf_op jit(solution)/shard_map/all_gather | solution.py:47
  52.3 1.9 convert_element_type.46
  54.2 0.0 copy-start.1
  54.2 0.6 copy.14
  54.9 0.9 bitcast_reduce_fusion
  55.8 55.9 %all-to-all-done = bf16[8,896,512]{1,2,0:T(8,128)(2,1)} async-done(((bf16[8,896,512]{1,2,0:T(8,128)(2,1)}), bf16[8,896,512]{1,2,0:T(8,128)(2,1)}, u32[]{:S(2)}, u32[]{:S(2)}) %all-to-all-start) | async-done | bytes 7340064 | tf_op jit(solution)/shard_map/all_to_all | solution.py:7
  111.7 80.2 %all-gather.4.cloned.1.call-done = bf16[1792,4096]{1,0:T(8,128)(2,1)} async-done(((bf16[1792,128]{1,0:T(8,128)(2,1)}), bf16[1792,4096]{1,0:T(8,128)(2,1)}) %all-gather.4.cloned.1.call-update) | async-done | bytes 14680080 | tf_op jit(solution)/shard_map/all_gather | solution.py:53
  191.9 0.0 copy-done.1
  191.9 0.0 copy-start.2
  191.9 22.1 %fusion.4 = f32[896,64,1]{0,1,2:T(8,128)S(1)} fusion(bf16[1792,64]{0,1:T(8,128)(2,1)S(1)} %copy-done.1, bf16[896,1792]{1,0:T(8,128)(2,1)} %param.10, bf16[896,4096]{0,1:T(8,128)(2,1)} %bitcast.2, bf16[1792,4096]{1,0:T(8,128)(2,1)} %all-gather.4.cloned.1.call-done), kind=kOutput, calls=%fused_computation.7 | convolution fusion | flops 13363675136 | bytes 25690112 | tf_op jit(solution)/shard_map/dot_general | solution.py:58
  214.0 1.7 fusion.1
  215.7 0.1 reshape.95
  215.8 0.7 copy.16
  216.5 4.3 %all-to-all-start.1 = ((f32[8,8,512]{2,1,0:T(8,128)}), f32[8,8,512]{2,1,0:T(8,128)S(1)}, u32[]{:S(2)}, u32[]{:S(2)}) async-start(f32[8,8,512]{2,1,0:T(8,128)} %bitcast.24), calls=%async_computation.1 | async-start | bytes 262144 | tf_op jit(solution)/shard_map/all_to_all | solution.py:62
  220.8 0.0 copy-done.2
  220.8 0.1 dynamic_slice.3
  220.9 6.1 %all-to-all-done.1 = f32[8,8,512]{2,1,0:T(8,128)S(1)} async-done(((f32[8,8,512]{2,1,0:T(8,128)}), f32[8,8,512]{2,1,0:T(8,128)S(1)}, u32[]{:S(2)}, u32[]{:S(2)}) %all-to-all-start.1) | async-done | bytes 131104 | tf_op jit(solution)/shard_map/all_to_all | solution.py:62
  226.9 0.2 fusion.3
  227.2 17.7 %all_to_all.19 = bf16[32,8,512]{2,1,0:T(8,128)(2,1)S(1)} all-to-all(bf16[32,8,512]{2,1,0:T(8,128)(2,1)S(1)} %fusion.3), channel_id=1, replica_groups=mesh['dp'=32,'tensor'=8] {'dp'}, dimensions={0} | all-to-all | bytes 524288 | tf_op jit(solution)/shard_map/all_to_all | solution.py:33
  244.9 0.7 reshape.96
  (5 shorter events, 0.1 us)
Async XLA Ops:
  6.5 1.2 copy-start
  6.5 45.8 %all-gather.6.cloned.1.call-start = ((), (), s32[]{:S(2)}) async-start(), calls=%async_computation.4 | async-start | bytes 2064384 | tf_op jit(solution)/shard_map/all_gather | solution.py:47
  9.7 182.2 %all-gather.4.cloned.1.call-start = ((), (), s32[]{:S(2)}) async-start(), calls=%async_computation.3 | async-start | bytes 15138816 | tf_op jit(solution)/shard_map/all_gather | solution.py:53
  15.9 5.0 %copy-start.3 = (s32[1,8]{1,0:T(1,128)S(1)}, s32[1,8]{1,0:T(1,128)}, u32[]{:S(2)}) copy-start(s32[1,8]{1,0:T(1,128)} %param.14) | copy-start | bytes 100
  15.9 95.7 %all-to-all-start = ((bf16[8,896,512]{1,2,0:T(8,128)(2,1)}), bf16[8,896,512]{1,2,0:T(8,128)(2,1)}, u32[]{:S(2)}, u32[]{:S(2)}) async-start(bf16[8,896,512]{1,2,0:T(8,128)(2,1)} %stack.2), calls=%async_computation | async-start | bytes 14680064 | tf_op jit(solution)/shard_map/all_to_all | solution.py:7
  54.2 137.7 %copy-start.1 = (bf16[1792,64]{0,1:T(8,128)(2,1)S(1)}, bf16[1792,64]{0,1:T(8,128)(2,1)}, u32[]{:S(2)}) copy-start(bf16[1792,64]{0,1:T(8,128)(2,1)} %param.13) | copy-start | bytes 688132
  191.9 28.9 %copy-start.2 = (s32[256]{0:T(256)S(1)}, s32[256]{0:T(256)}, u32[]{:S(2)}) copy-start(s32[256]{0:T(256)} %param.15) | copy-start | bytes 3076
  216.5 10.4 %all-to-all-start.1 = ((f32[8,8,512]{2,1,0:T(8,128)}), f32[8,8,512]{2,1,0:T(8,128)S(1)}, u32[]{:S(2)}, u32[]{:S(2)}) async-start(f32[8,8,512]{2,1,0:T(8,128)} %bitcast.24), calls=%async_computation.1 | async-start | bytes 262144 | tf_op jit(solution)/shard_map/all_to_all | solution.py:62
Sparse Core Ops, SparseCore 0:
  9.8 42.4 all-gather.5
  54.8 137.0 all-gather.3
